TPU v7x, 512 devices: a whole 4x4x16 slice. The times are simulated.
512 devices in a mesh: req: 32 (over z_lo, x), seq: 16 (over y, z_hi, core).
Axes of the slice: x: 4, y: 4, z: 16 (z_hi: 2, z_lo: 8; z = z_hi * 8 + z_lo), core: 2. Of those that a mesh axis runs over, the one named last changes fastest.
Arguments:
- query_block: bfloat16 [32, 16, 64, 10240], P('req', 'seq'), may hold values from -40 to 40
- k_cache: bfloat16 [32, 10752, 1024], P('req', 'seq'), may hold values from -40 to 40
- v_cache: bfloat16 [32, 10752, 1024], P('req', 'seq'), may hold values from -6 to 6
- ctx_len: int32 [32], P('req'), may hold values from 5376 to 10752, as said below
- host: int32 [32], P('req'), may hold values from 0 to 15
Outputs:
- attended: bfloat16 [32, 16, 64, 8192], P('req', 'seq')
Inputs may be any that keep to these rules, and one draw needn't show every extreme that they name: ctx_len lies between 5376 and 10752; the largest equals 10752.
All inputs are finite; a program needn't handle non-finite values.
Results may differ from a plain program's by a relative error of at most 0.0046.
Values may be sent and summed in bfloat16 or wider, within the bound.
A program may use at most 128 MiB of HBM per device.

v0:
```python
import math

import jax
import jax.numpy as jnp
from jax import lax
from jax.sharding import PartitionSpec as P

HQ = 64
HK = 8
DH = 128


NEG_FILL = -1e30


def broadcast(value, axis, source):
    kept = jnp.where(lax.axis_index(axis) == source, value, 0).astype(value.dtype)
    return lax.psum(kept, axis)


def local(query_block, k_cache, v_cache, ctx_len, host):
    group = HQ // HK
    ctx_rows = k_cache.shape[1]
    rows = query_block.shape[2]
    position = lax.axis_index("seq")
    root = host[0]
    is_host = position == root
    mine = query_block[0, 0]
    block = broadcast(mine, "seq", root)
    queries = block[:, : HQ * DH].reshape(rows, HK, group, DH)
    new_keys = block[:, HQ * DH : (HQ + HK) * DH].reshape(rows, HK, DH)
    new_values = block[:, (HQ + HK) * DH :].reshape(rows, HK, DH)
    ctx_keys = k_cache[0].reshape(ctx_rows, HK, DH)
    ctx_values = v_cache[0].reshape(ctx_rows, HK, DH)
    scale = 1.0 / math.sqrt(DH)
    ctx_scores = (
        jnp.einsum("qhgd,khd->hgqk", queries, ctx_keys, preferred_element_type=jnp.float32) * scale
    )
    new_scores = (
        jnp.einsum("qhgd,khd->hgqk", queries, new_keys, preferred_element_type=jnp.float32) * scale
    )
    places = position * ctx_rows + jnp.arange(ctx_rows, dtype=jnp.int32)
    valid = places < ctx_len[0]
    causal = (jnp.arange(rows)[:, None] >= jnp.arange(rows)[None, :]) & is_host
    ctx_masked = jnp.where(valid, ctx_scores, NEG_FILL)
    new_masked = jnp.where(causal, new_scores, NEG_FILL)
    ctx_top = jnp.max(ctx_masked, axis=-1)
    new_top = jnp.max(new_masked, axis=-1)
    ctx_weights = jnp.where(valid, jnp.exp(ctx_masked - ctx_top[..., None]), 0.0)
    new_weights = jnp.where(causal, jnp.exp(new_masked - new_top[..., None]), 0.0)
    local_top = jnp.maximum(ctx_top, new_top)
    ctx_factor = jnp.exp(ctx_top - local_top)
    new_factor = jnp.exp(new_top - local_top)
    local_total = (
        jnp.sum(ctx_weights, axis=-1) * ctx_factor + jnp.sum(new_weights, axis=-1) * new_factor
    )
    ctx_sum = jnp.einsum(
        "hgqk,khd->hgqd",
        ctx_weights.astype(jnp.bfloat16),
        ctx_values,
        preferred_element_type=jnp.float32,
    )
    new_sum = jnp.einsum(
        "hgqk,khd->hgqd",
        new_weights.astype(jnp.bfloat16),
        new_values,
        preferred_element_type=jnp.float32,
    )
    local_sum = ctx_sum * ctx_factor[..., None] + new_sum * new_factor[..., None]
    global_top = lax.pmax(local_top, "seq")
    factor = jnp.exp(local_top - global_top)
    total, summed = lax.psum((local_total * factor, local_sum * factor[..., None]), "seq")
    result = summed / total[..., None]
    result = jnp.transpose(result, (2, 0, 1, 3)).reshape(rows, HQ * DH).astype(jnp.bfloat16)
    result = jnp.where(is_host, result, jnp.zeros((), jnp.bfloat16))
    return result[None, None]


def solution(mesh):
    return jax.shard_map(
        local,
        mesh=mesh,
        in_specs=(
            P("req", "seq", None, None),
            P("req", "seq", None),
            P("req", "seq", None),
            P("req"),
            P("req"),
        ),
        out_specs=P("req", "seq", None, None),
        check_vma=False,
    )
```

profile of v0, /device:TPU:102, one launch (start us, length us, event | category | flops | bytes accessed | tf_op | source)
XLA Modules:
  0.0 821.1 jit_solution(548020244626724786)
XLA Ops:
  6.5 0.0 copy-start
  6.5 0.0 all-reduce.3.cloned.1.call-start
  7.3 2.5 select_bitcast_fusion
  9.8 0.0 all-reduce.3.cloned.1.call-update
  9.8 0.0 all-reduce.5.cloned.1.call-start
  10.5 0.0 copy-done
  10.5 0.4 copy.82
  10.9 2.8 copy.83
  13.7 286.5 %all-reduce.3.cloned.1.call-done = bf16[64,10240]{1,0:T(8,128)(2,1)} async-done(((bf16[64,10240]{1,0:T(8,128)(2,1)}), bf16[64,10240]{1,0:T(8,128)(2,1)}) %all-reduce.3.cloned.1.call-update) | async-done | bytes 1310736 | tf_op jit(solution)/shard_map/psum | solution.py:18
  300.2 1.3 slice_bitcast_fusion
  301.5 0.3 copy.81
  301.8 5.8 bitcast_reduce_fusion
  307.6 0.1 copy.63
  307.7 11.5 %fusion.2 = (f32[8,8,64]{1,2,0:T(8,128)S(1)}, bf16[8,8,64,672]{3,1,2,0:T(8,128)(2,1)}) fusion(f32[8,64,8,672]{3,2,1,0:T(8,128)} %get-tuple-element.14, f32[8,8,64]{1,2,0:T(8,128)S(1)} %get-tuple-element.13, pred[672]{0:T(1024)(128)(4,1)S(1)} %add_compare_fusion), kind=kLoop, calls=%fused_computation.5 | loop fusion | flops 16510976 | bytes 16548512 | tf_op jit(solution)/shard_map/reduce_sum | solution.py:55
  319.2 1.6 slice_bitcast_fusion.1
  320.8 0.7 copy.66
  321.5 1.6 fusion.6
  323.1 0.0 copy-start.1
  323.1 1.3 fusion.7
  324.4 0.6 max.12
  325.0 130.6 %pmax.7 = f32[8,8,64]{2,1,0:T(8,128)} all-reduce(f32[8,8,64]{2,1,0:T(8,128)} %max.12), channel_id=1, replica_groups=mesh['req'=32,'seq'=16] {'seq'}, use_global_device_ids=true, to_apply=%region_3.4 | all-reduce | flops 4096 | bytes 32768 | tf_op jit(solution)/shard_map/pmax | solution.py:70
  455.6 0.9 copy.85
  456.6 0.0 copy-done.1
  456.6 0.0 copy-start.2
  456.6 0.0 copy-start.3
  456.6 0.0 copy-start.4
  456.6 0.0 copy-start.5
  456.6 4.6 fusion.4
  461.2 0.0 copy-done.2
  461.2 0.0 copy-done.3
  461.2 0.0 copy-done.4
  461.3 0.0 copy-done.5
  461.3 3.5 add_multiply_fusion
  464.8 0.0 all-reduce.5.cloned.1.call-update
  464.8 133.5 %psum.23 = f32[8,8,64]{2,1,0:T(8,128)S(1)} all-reduce(f32[8,8,64]{2,1,0:T(8,128)S(1)} %get-tuple-element.5), channel_id=1, replica_groups=mesh['req'=32,'seq'=16] {'seq'}, use_global_device_ids=true, to_apply=%region_7.8 | all-reduce | flops 4096 | bytes 32768 | tf_op jit(solution)/shard_map/psum | solution.py:72
  598.3 212.0 %all-reduce.5.cloned.1.call-done = f32[8,8,64,128]{3,2,1,0:T(8,128)} async-done(((f32[8,8,64,128]{3,2,1,0:T(8,128)}), f32[8,8,64,128]{3,2,1,0:T(8,128)}) %all-reduce.5.cloned.1.call-update) | async-done | bytes 2097168 | tf_op jit(solution)/shard_map/psum | solution.py:72
  810.3 1.9 select_bitcast_fusion.1
  812.3 0.7 copy.67
  813.0 1.3 select_n.60
  (4 shorter events, 0.1 us)
Async XLA Ops:
  6.5 4.0 copy-start
  6.5 293.7 %all-reduce.3.cloned.1.call-start = ((), (), s32[]{:S(2)}) async-start(), calls=%async_computation | async-start | bytes 2621440 | tf_op jit(solution)/shard_map/psum | solution.py:18
  9.8 800.5 %all-reduce.5.cloned.1.call-start = ((), (), s32[]{:S(2)}) async-start(), calls=%async_computation.1 | async-start | bytes 4194304 | tf_op jit(solution)/shard_map/psum | solution.py:72
  323.1 133.5 %copy-start.1 = (bf16[84,8,8,128]{3,2,1,0:T(8,128)(2,1)S(1)}, bf16[84,8,8,128]{3,2,1,0:T(8,128)(2,1)}, u32[]{:S(2)}) copy-start(bf16[84,8,8,128]{3,2,1,0:T(8,128)(2,1)} %copy.83) | copy-start | bytes 4128772
  456.6 4.7 copy-start.2
  456.6 4.7 copy-start.3
  456.6 4.7 copy-start.4
  456.6 4.7 copy-start.5
Sparse Core Ops, SparseCore 0:
  10.3 289.8 all-reduce.2
  465.0 345.3 all-reduce.4
where the time goes:
time: 821 us
  waiting for transfers between devices  499 us (61%)
  blocking collectives  264 us (32%)
  other arithmetic  17.8 us (2%)
  matrix products  15.5 us (2%)
  between operations  15 us (2%)
  local copies, waits for them, and re-layouts  10.1 us (1%)
    psum x1, waiting for transfers between devices, broadcast(): return lax.psum(kept, axis)  286 us
    psum x1, waiting for transfers between devices, local(): lax.psum((local_total * factor, local_sum * factor[..., None]), 'seq')  212 us
    psum x1, blocking collectives, local(): lax.psum((local_total * factor, local_sum * factor[..., None]), 'seq')  133 us
    pmax x1, blocking collectives, local(): global_top = lax.pmax(local_top, 'seq')  131 us
  transfers between devices with their start and end apart: 2, of which 2 were waited for; matrix products, arithmetic and copies ran while one was open for 0% of the time, Pallas kernels for 0%

commit v1 on v0

v1 whole, which is shorter than its diff:
```python
import functools
import math

import jax
import jax.numpy as jnp
from jax import lax
from jax.experimental import pallas as pl
from jax.experimental.pallas import tpu as pltpu
from jax.sharding import PartitionSpec as P

HQ = 64
HK = 8
DH = 128
ROWS = 64
NY = 4
CHUNKS = 4
HP = 2
PIECE = HP * DH
LANES = HP * ROWS
HALF = NY * LANES
HALF_COLS = NY * PIECE
CHUNK_COLS = 2 * HALF_COLS
UNIT = 256
SCALE2 = math.log2(math.e) / math.sqrt(DH)
NEG = -1e30
FLOOR = -1e20
ABSENT = -2e20

CORE_Q, Y_Q, Z_Q, Y_QALL, CORE_QALL, CORE_O, Y_O, Z_O, Y_OALL, CORE_OALL = 0, 1, 4, 5, 8, 9, 10, 13, 14, 17
STAGES = 18


def three_parts(x):
    high = x.astype(jnp.bfloat16).astype(jnp.float32)
    rest = x - high
    mid = rest.astype(jnp.bfloat16).astype(jnp.float32)
    low = (rest - mid).astype(jnp.bfloat16).astype(jnp.float32)
    return high, mid, low


def pack_stats(top, total):
    width = top.shape[1]
    row = lax.broadcasted_iota(jnp.int32, (16, width), 0)
    out = jnp.zeros((16, width), jnp.float32)
    for at, part in enumerate(three_parts(top) + three_parts(total)):
        out = jnp.where(row == at, part, out)
    return out.astype(jnp.bfloat16)


def unpack_stats(packed):
    s = packed.astype(jnp.float32)
    return s[0:1] + s[1:2] + s[2:3], s[3:4] + s[4:5] + s[5:6]


def merge(parts):
    top = functools.reduce(jnp.maximum, [p[0] for p in parts])
    factors = [jnp.exp2((p[0] - top) * SCALE2) for p in parts]
    total = functools.reduce(jnp.add, [p[1] * f for p, f in zip(parts, factors)])
    summed = functools.reduce(jnp.add, [p[2] * f for p, f in zip(parts, factors)])
    return top, total, summed


def block_attention(keys, values, queries, keep):
    scores = lax.dot_general(keys, queries, (((1,), (1,)), ((), ())), preferred_element_type=jnp.float32)
    scores = jnp.where(keep, scores, NEG)
    top = jnp.maximum(jnp.max(scores, axis=0, keepdims=True), FLOOR)
    weights = jnp.exp2((scores - top) * SCALE2)
    total = jnp.sum(weights, axis=0, keepdims=True)
    summed = lax.dot_general(
        values, weights.astype(jnp.bfloat16), (((0,), (0,)), ((), ())), preferred_element_type=jnp.float32
    )
    return top, total, summed


def kernel(
    ctx_ref, host_ref, q_hbm, k_hbm, v_hbm, o_hbm,
    q_all, k_all, v_all, core_q, y_src, y_q, z_q, q_full,
    new_sum, new_stats, o_src, o_core, kept, y_osrc, y_o, half_o, z_osrc, z_o, o_full,
    local_sem, send_sem, recv_sem,
):
    context = k_hbm.shape[0]
    seq = lax.axis_index("seq")
    core = lax.rem(seq, 2)
    zhi = lax.rem(lax.div(seq, 2), 2)
    y = lax.div(seq, 4)
    other = 1 - core
    sibling = seq + 1 - 2 * core
    across = seq + 2 - 4 * zhi

    host = host_ref[0]
    host_core = lax.rem(host, 2)
    host_z = lax.rem(lax.div(host, 2), 2)
    host_y = lax.div(host, 4)

    def pick(index, values):
        out = values[0]
        for at in range(1, len(values)):
            out = lax.select(index == at, values[at], out)
        return out

    def cols(start, size):
        return pl.ds(pl.multiple_of(start, 128), size)

    def y_of(k):
        return lax.rem(y + k, NY)

    def beside(k):
        return lax.rem(seq + 4 * k, 16)

    def remote(src, dst, stage, s, to):
        return pltpu.make_async_remote_copy(
            src_ref=src,
            dst_ref=dst,
            send_sem=send_sem.at[stage, s],
            recv_sem=recv_sem.at[stage, s],
            device_id={"seq": to},
            device_id_type=pl.DeviceIdType.MESH,
        )

    def send_core_q(s):
        return remote(
            q_hbm.at[:, cols(s * CHUNK_COLS + other * HALF_COLS, HALF_COLS)], core_q.at[s, core], CORE_Q, s, sibling
        )

    def send_y_q(s, k):
        return remote(y_src.at[s, y_of(k)], y_q.at[s, y], Y_Q + k - 1, s, beside(k))

    def send_z_q(s):
        return remote(z_q.at[s, zhi], z_q.at[s, zhi], Z_Q, s, across)

    def send_y_qall(s, k):
        piece = core * NY + y
        return remote(q_full.at[s, piece], q_full.at[s, piece], Y_QALL + k - 1, s, beside(k))

    def send_core_qall(s):
        pieces = q_full.at[s, pl.ds(core * NY, NY)]
        return remote(pieces, pieces, CORE_QALL, s, sibling)

    def send_core_o(s):
        return remote(o_src.at[s], o_core.at[s], CORE_O, s, sibling)

    def send_y_o(s, k):
        return remote(y_osrc.at[s, y_of(k)], y_o.at[s, y], Y_O + k - 1, s, beside(k))

    def send_z_o(s):
        return remote(z_osrc.at[s], z_o.at[s], Z_O, s, across)

    def send_y_oall(s, k):
        piece = o_full.at[s, :, cols((other * NY + y) * PIECE, PIECE)]
        return remote(piece, piece, Y_OALL + k - 1, s, beside(k))

    def send_core_oall(s):
        pieces = o_full.at[s, :, cols(other * HALF_COLS, HALF_COLS)]
        return remote(pieces, pieces, CORE_OALL, s, sibling)

    def write_out(s):
        return pltpu.make_async_copy(o_full.at[s], o_hbm.at[:, cols(s * CHUNK_COLS, CHUNK_COLS)], local_sem.at[4 + s])

    def own_q(s):
        return pltpu.make_async_copy(
            q_hbm.at[:, cols(s * CHUNK_COLS + core * HALF_COLS, HALF_COLS)], core_q.at[s, core], local_sem.at[4 + s]
        )

    loads = [
        pltpu.make_async_copy(src, dst, local_sem.at[at])
        for at, (src, dst) in enumerate(((q_hbm, q_all), (k_hbm, k_all), (v_hbm, v_all)))
    ]
    for s in range(CHUNKS):
        own_q(s).start()
    for copy in loads:
        copy.start()

    barrier = pltpu.get_barrier_semaphore()
    for to in (across, beside(2), beside(1), beside(3), sibling):
        pl.semaphore_signal(barrier, inc=1, device_id={"seq": to}, device_id_type=pl.DeviceIdType.MESH)
    pl.semaphore_wait(barrier, 5)

    @pl.loop(0, CHUNKS)
    def _(s):
        send_core_q(s).start()

    @pl.loop(0, CHUNKS)
    def _(s):
        own_q(s).wait()
        send_core_q(s).wait_recv()
        for at in range(NY):
            piece = slice(at * PIECE, (at + 1) * PIECE)
            y_src[s, at] = pick(host_core, [core_q[s, c, :, piece] for c in range(2)])
        for k in (2, 1, 3):
            send_y_q(s, k).start()
        y_q[s, y] = y_src[s, y]

    @pl.loop(0, CHUNKS)
    def _(s):
        for k in (1, 3, 2):
            send_y_q(s, k).wait_recv()
        z_q[s, zhi] = pick(host_y, [y_q[s, at] for at in range(NY)])
        send_z_q(s).start()

    for copy in loads:
        copy.wait()
    is_host = jnp.broadcast_to(host, (1, HALF)) == jnp.broadcast_to(seq, (1, HALF))
    causal = lax.broadcasted_iota(jnp.int32, (ROWS, HALF), 0) <= lax.rem(
        lax.broadcasted_iota(jnp.int32, (ROWS, HALF), 1), ROWS
    )

    @pl.loop(0, HK)
    def _(g):
        queries = jnp.concatenate(
            [q_all[:, cols(g * HALF_COLS + h * DH, DH)] for h in range(HQ // HK)], axis=0
        )
        new_keys = q_all[:, cols(HQ * DH + g * DH, DH)]
        new_values = q_all[:, cols((HQ + HK) * DH + g * DH, DH)]
        top, total, summed = block_attention(new_keys, new_values, queries, causal)
        new_sum[g] = summed
        new_stats[g, 0:1] = jnp.where(is_host, top, ABSENT)
        new_stats[g, 1:2] = total

    valid = ctx_ref[0] - seq * context

    def attend(s, half, unit):
        g = 2 * s + half
        at = unit * UNIT
        keys = k_all[:, cols(g * DH, DH)]
        values = v_all[:, cols(g * DH, DH)]
        heads = range(at // ROWS, (at + UNIT) // ROWS)
        queries = jnp.concatenate(
            [q_full[s, half * NY + h // HP, :, (h % HP) * DH : (h % HP + 1) * DH] for h in heads], axis=0
        )
        keep = lax.broadcasted_iota(jnp.int32, (context, UNIT), 0) < valid
        here = block_attention(keys, values, queries, keep)
        new = (new_stats[g, 0:1, at : at + UNIT], new_stats[g, 1:2, at : at + UNIT], new_sum[g, :, at : at + UNIT])
        return merge([here, new])

    def gather_q(s):
        send_z_q(s).wait_recv()
        q_full[s, core * NY + y] = pick(host_z, [z_q[s, at] for at in range(2)])
        for k in (2, 1, 3):
            send_y_qall(s, k).start()

    def compute(s):
        for k in (1, 3, 2):
            send_y_qall(s, k).wait_recv()
        send_core_qall(s).start()
        for unit in range(HALF // UNIT):
            top, total, summed = attend(s, core, unit)
            at = unit * UNIT
            o_src[s, 0:DH, at : at + UNIT] = summed
            o_src[s, DH : DH + 1, at : at + UNIT] = top
            o_src[s, DH + 1 : DH + 2, at : at + UNIT] = total
        send_core_o(s).start()
        send_core_qall(s).wait_recv()
        mine = [attend(s, other, unit) for unit in range(HALF // UNIT)]
        send_core_o(s).wait_recv()
        for unit, part in enumerate(mine):
            at = unit * UNIT
            beside_it = (
                o_core[s, DH : DH + 1, at : at + UNIT],
                o_core[s, DH + 1 : DH + 2, at : at + UNIT],
                o_core[s, 0:DH, at : at + UNIT],
            )
            top, total, summed = merge([part, beside_it])
            packed = pack_stats(top, total)
            for sub in range(UNIT // LANES):
                lanes = slice(sub * LANES, (sub + 1) * LANES)
                piece = unit * (UNIT // LANES) + sub
                y_osrc[s, piece, 0:DH] = summed[:, lanes].astype(jnp.bfloat16)
                y_osrc[s, piece, DH : DH + 16] = packed[:, lanes]
                kept[s, piece, 0:DH] = summed[:, lanes]
                kept[s, piece, DH : DH + 1] = top[:, lanes]
                kept[s, piece, DH + 1 : DH + 2] = total[:, lanes]
        for k in (2, 1, 3):
            send_y_o(s, k).start()

    def arrived(ref, *at):
        top, total = unpack_stats(ref[(*at, slice(DH, DH + 16))])
        return top, total, ref[(*at, slice(0, DH))].astype(jnp.float32)

    def sum_y(s):
        for k in (1, 3, 2):
            send_y_o(s, k).wait_recv()
        own = (kept[s, y, DH : DH + 1], kept[s, y, DH + 1 : DH + 2], kept[s, y, 0:DH])
        top, total, summed = merge([own] + [arrived(y_o, s, y_of(k)) for k in (1, 2, 3)])
        z_osrc[s, 0:DH] = summed.astype(jnp.bfloat16)
        z_osrc[s, DH : DH + 16] = pack_stats(top, total)
        send_z_o(s).start()
        half_o[s, 0:DH] = summed
        half_o[s, DH : DH + 1] = top
        half_o[s, DH + 1 : DH + 2] = total

    @pl.loop(0, CHUNKS + 3)
    def _(t):
        @pl.when(t < CHUNKS)
        def _():
            gather_q(t)

        @pl.when((t >= 1) & (t <= CHUNKS))
        def _():
            compute(t - 1)

        @pl.when(t >= 3)
        def _():
            sum_y(t - 3)

    def finish(s):
        send_z_o(s).wait_recv()
        own = (half_o[s, DH : DH + 1], half_o[s, DH + 1 : DH + 2], half_o[s, 0:DH])
        _, total, summed = merge([own, arrived(z_o, s)])
        result = jnp.transpose(summed / total).astype(jnp.bfloat16)
        for h in range(HP):
            o_full[s, :, cols((other * NY + y) * PIECE + h * DH, DH)] = result[h * ROWS : (h + 1) * ROWS]
        for k in (2, 1, 3):
            send_y_oall(s, k).start()

    def gather_o(s):
        for k in (1, 3, 2):
            send_y_oall(s, k).wait_recv()
        send_core_oall(s).start()
        send_core_oall(s).wait_recv()
        write_out(s).start()

    @pl.loop(0, CHUNKS + 1)
    def _(t):
        @pl.when(t < CHUNKS)
        def _():
            finish(t)

        @pl.when(t >= 1)
        def _():
            gather_o(t - 1)

    @pl.loop(0, CHUNKS)
    def _(s):
        for copy in (send_core_q, send_z_q, send_core_qall, send_core_o, send_z_o, send_core_oall):
            copy(s).wait_send()
        for copy in (send_y_q, send_y_qall, send_y_o, send_y_oall):
            for k in (1, 2, 3):
                copy(s, k).wait_send()
        write_out(s).wait()


def attention(query_block, keys, values, ctx_len, host):
    context, width = keys.shape
    bf16, f32 = jnp.bfloat16, jnp.float32
    vmem = pltpu.VMEM
    return pl.pallas_call(
        kernel,
        out_shape=jax.ShapeDtypeStruct((ROWS, HQ * DH), bf16),
        in_specs=[pl.BlockSpec(memory_space=pltpu.SMEM)] * 2 + [pl.BlockSpec(memory_space=pl.ANY)] * 3,
        out_specs=pl.BlockSpec(memory_space=pl.ANY),
        scratch_shapes=[
            vmem(query_block.shape, bf16),
            vmem((context, width), bf16),
            vmem((context, width), bf16),
            vmem((CHUNKS, 2, ROWS, HALF_COLS), bf16),
            vmem((CHUNKS, NY, ROWS, PIECE), bf16),
            vmem((CHUNKS, NY, ROWS, PIECE), bf16),
            vmem((CHUNKS, 2, ROWS, PIECE), bf16),
            vmem((CHUNKS, 2 * NY, ROWS, PIECE), bf16),
            vmem((HK, DH, HALF), f32),
            vmem((HK, 8, HALF), f32),
            vmem((CHUNKS, DH + 8, HALF), f32),
            vmem((CHUNKS, DH + 8, HALF), f32),
            vmem((CHUNKS, NY, DH + 8, LANES), f32),
            vmem((CHUNKS, NY, DH + 16, LANES), bf16),
            vmem((CHUNKS, NY, DH + 16, LANES), bf16),
            vmem((CHUNKS, DH + 8, LANES), f32),
            vmem((CHUNKS, DH + 16, LANES), bf16),
            vmem((CHUNKS, DH + 16, LANES), bf16),
            vmem((CHUNKS, ROWS, CHUNK_COLS), bf16),
            pltpu.SemaphoreType.DMA((4 + CHUNKS,)),
            pltpu.SemaphoreType.DMA((STAGES, CHUNKS)),
            pltpu.SemaphoreType.DMA((STAGES, CHUNKS)),
        ],
        compiler_params=pltpu.CompilerParams(
            collective_id=0, has_side_effects=True, vmem_limit_bytes=52 * 1024 * 1024
        ),
        name="context_attention",
    )(ctx_len, host, query_block, keys, values)


def local(query_block, k_cache, v_cache, ctx_len, host):
    result = attention(query_block[0, 0], k_cache[0], v_cache[0], ctx_len, host)
    result = jnp.where(lax.axis_index("seq") == host[0], result, jnp.zeros((), jnp.bfloat16))
    return result[None, None]


def solution(mesh):
    return jax.shard_map(
        local,
        mesh=mesh,
        in_specs=(
            P("req", "seq", None, None),
            P("req", "seq", None),
            P("req", "seq", None),
            P("req"),
            P("req"),
        ),
        out_specs=P("req", "seq", None, None),
        check_vma=False,
    )
```

time: 821 us -> 73.8 us (0.09)
  the two profiles are of different devices: /device:TPU:102 before, /device:TPU:37 now
where the time goes in v1:
time: 73.8 us; the launch traced here: 73.7 us
  Pallas kernels  71.4 us (97%)
  between operations  1.31 us (2%)
  other arithmetic  1.04 us (1%)
    pallas_call x1, Pallas kernels, attention(): pl.pallas_call(kernel, out_shape=jax.ShapeDtypeStruct((ROWS, HQ * DH), bf...  71.4 us

profile of v1, /device:TPU:37, one launch (start us, length us, event | category | flops | bytes accessed | tf_op | source)
XLA Modules:
  0.0 73.7 jit_solution(6900866794618016824)
XLA Ops:
  1.3 71.4 %context_attention.1 = bf16[64,8192]{1,0:T(8,128)(2,1)S(1)} custom-call(s32[1]{0:T(128)S(6)} %copy.6.ctx_ref, s32[1]{0:T(128)} %copy.7.host_ref, bf16[64,10240]{1,0:T(8,128)(2,1)} %bitcast.9, bf16[672,1024]{1,0:T(8,128)(2,1)} %bitcast.7, bf16[672,1024]{1,0:T(8,128)(2,1)} %bitcast.8), custom_call_target="tpu_custom_call" | custom-call | tf_op jit(solution)/shard_map/context_attention/pallas_call | solution.py:346
  72.7 1.0 %select_bitcast_fusion = bf16[1,1,64,8192]{3,2,1,0:T(8,128)(2,1)} fusion(bf16[64,8192]{1,0:T(8,128)(2,1)S(1)} %context_attention.1, pred[]{:T(512)S(6)} %eq.3), kind=kLoop, calls=%fused_computation | loop fusion | flops 524288 | bytes 2097153 | tf_op jit(solution)/shard_map/broadcast_in_dim | solution.py:385

commit v2 on v1

v2 whole, which is shorter than its diff:
```python
import functools
import math

import jax
import jax.numpy as jnp
from jax import lax
from jax.experimental import pallas as pl
from jax.experimental.pallas import tpu as pltpu
from jax.sharding import PartitionSpec as P

HQ = 64
HK = 8
DH = 128
ROWS = 64
NY = 4
CHUNKS = 8
HALF_COLS = HQ // HK * DH // 2
CHUNK_COLS = 2 * HALF_COLS
LANES = 256
BLOCK = 128
DEPTH = DH // 2
SCALE2 = math.log2(math.e) / math.sqrt(DH)
NEG = -1e30
FLOOR = -1e20
ABSENT = -2e20

CORE_Q, Y_Q, Z_Q, Y_QALL, CORE_QALL, CORE_O, Y_O, Z_O, Y_OALL, CORE_OALL = 0, 1, 4, 5, 8, 9, 10, 13, 14, 17
STAGES = 18

AT_NEAR, AT_FAR, AT_SUM, AT_FINISH, AT_GATHER, AT_WRITE = 4, 5, 8, 16, 20, 22


def three_parts(x):
    high = x.astype(jnp.bfloat16).astype(jnp.float32)
    rest = x - high
    mid = rest.astype(jnp.bfloat16).astype(jnp.float32)
    low = (rest - mid).astype(jnp.bfloat16).astype(jnp.float32)
    return high, mid, low


def pack_stats(top, total):
    width = top.shape[1]
    row = lax.broadcasted_iota(jnp.int32, (16, width), 0)
    out = jnp.zeros((16, width), jnp.float32)
    for at, part in enumerate(three_parts(top) + three_parts(total)):
        out = jnp.where(row == at, part, out)
    return out.astype(jnp.bfloat16)


def unpack_stats(packed):
    s = packed.astype(jnp.float32)
    return s[0:1] + s[1:2] + s[2:3], s[3:4] + s[4:5] + s[5:6]


def merge(parts):
    top = functools.reduce(jnp.maximum, [p[0] for p in parts])
    factors = [jnp.exp2((p[0] - top) * SCALE2) for p in parts]
    total = functools.reduce(jnp.add, [p[1] * f for p, f in zip(parts, factors)])
    summed = functools.reduce(jnp.add, [p[2] * f for p, f in zip(parts, factors)])
    return top, total, summed


def weigh(keys, queries, keep):
    scores = lax.dot_general(keys, queries, (((1,), (1,)), ((), ())), preferred_element_type=jnp.float32)
    scores = jnp.where(keep, scores, NEG)
    top = jnp.maximum(jnp.max(scores, axis=0, keepdims=True), FLOOR)
    weights = jnp.exp2((scores - top) * SCALE2)
    return top, jnp.sum(weights, axis=0, keepdims=True), weights.astype(jnp.bfloat16)


def kernel(
    ctx_ref, host_ref, q_hbm, k_hbm, v_hbm, o_hbm,
    q_all, k_all, v_all, v_turned, core_q, y_src, y_q, z_q, q_full,
    new_sum, new_stats, o_src, o_core, kept, y_osrc, y_o, half_o, z_osrc, z_o, o_pieces, o_full,
    local_sem, send_sem, recv_sem,
):
    context = k_hbm.shape[0]
    seq = lax.axis_index("seq")
    core = lax.rem(seq, 2)
    zhi = lax.rem(lax.div(seq, 2), 2)
    y = lax.div(seq, 4)
    other = 1 - core
    sibling = seq + 1 - 2 * core
    across = seq + 2 - 4 * zhi

    host = host_ref[0]
    host_core = lax.rem(host, 2)
    host_z = lax.rem(lax.div(host, 2), 2)
    host_y = lax.div(host, 4)

    def pick(index, values):
        out = values[0]
        for at in range(1, len(values)):
            out = lax.select(index == at, values[at], out)
        return out

    def cols(start, size):
        return pl.ds(pl.multiple_of(start, 128), size)

    def y_of(k):
        return lax.rem(y + k, NY)

    def beside(k):
        return lax.rem(seq + 4 * k, 16)

    def remote(src, dst, stage, s, to):
        return pltpu.make_async_remote_copy(
            src_ref=src,
            dst_ref=dst,
            send_sem=send_sem.at[stage, s],
            recv_sem=recv_sem.at[stage, s],
            device_id={"seq": to},
            device_id_type=pl.DeviceIdType.MESH,
        )

    def send_core_q(s):
        return remote(
            q_hbm.at[:, cols(s * CHUNK_COLS + other * HALF_COLS, HALF_COLS)], core_q.at[s, core], CORE_Q, s, sibling
        )

    def send_y_q(s, k):
        return remote(y_src.at[s, y_of(k)], y_q.at[s, y], Y_Q + k - 1, s, beside(k))

    def send_z_q(s):
        return remote(z_q.at[s, zhi], z_q.at[s, zhi], Z_Q, s, across)

    def send_y_qall(s, k):
        piece = q_full.at[s, core, y]
        return remote(piece, piece, Y_QALL + k - 1, s, beside(k))

    def send_core_qall(s):
        return remote(q_full.at[s, core], q_full.at[s, core], CORE_QALL, s, sibling)

    def send_core_o(s):
        return remote(o_src.at[s], o_core.at[s], CORE_O, s, sibling)

    def send_y_o(s, k):
        return remote(y_osrc.at[s, y_of(k)], y_o.at[s, y], Y_O + k - 1, s, beside(k))

    def send_z_o(s):
        return remote(z_osrc.at[s], z_o.at[s], Z_O, s, across)

    def send_y_oall(s, k):
        piece = o_pieces.at[s, other, y]
        return remote(piece, piece, Y_OALL + k - 1, s, beside(k))

    def send_core_oall(s):
        return remote(o_pieces.at[s, other], o_pieces.at[s, other], CORE_OALL, s, sibling)

    def write_out(s):
        return pltpu.make_async_copy(o_full.at[s], o_hbm.at[:, cols(s * CHUNK_COLS, CHUNK_COLS)], local_sem.at[4 + s])

    def own_q(s):
        return pltpu.make_async_copy(
            q_hbm.at[:, cols(s * CHUNK_COLS + core * HALF_COLS, HALF_COLS)], core_q.at[s, core], local_sem.at[4 + s]
        )

    loads = [
        pltpu.make_async_copy(src, dst, local_sem.at[at])
        for at, (src, dst) in enumerate(((q_hbm, q_all), (k_hbm, k_all), (v_hbm, v_all)))
    ]
    barrier = pltpu.get_barrier_semaphore()

    def greet(to):
        pl.semaphore_signal(barrier, inc=1, device_id={"seq": to}, device_id_type=pl.DeviceIdType.MESH)

    for to in (beside(2), beside(1), beside(3), sibling):
        greet(to)
    for s in range(CHUNKS):
        own_q(s).start()
    for copy in loads:
        copy.start()

    @pl.when(zhi == 0)
    def _():
        pl.semaphore_wait(barrier, 4)
        greet(across)

    @pl.when(zhi == 1)
    def _():
        pl.semaphore_wait(barrier, 5)
        greet(across)

    @pl.loop(0, CHUNKS)
    def _(s):
        send_core_q(s).start()

    @pl.loop(0, CHUNKS)
    def _(s):
        own_q(s).wait()
        send_core_q(s).wait_recv()
        for at in range(NY):
            piece = slice(at * DH, (at + 1) * DH)
            y_src[s, at] = pick(host_core, [core_q[s, c, :, piece] for c in range(2)])
        for k in (2, 1, 3):
            send_y_q(s, k).start()
        y_q[s, y] = y_src[s, y]

    for copy in loads:
        copy.wait()
    is_host = jnp.broadcast_to(host, (1, 2 * LANES)) == jnp.broadcast_to(seq, (1, 2 * LANES))
    causal = lax.broadcasted_iota(jnp.int32, (ROWS, 2 * LANES), 0) <= lax.rem(
        lax.broadcasted_iota(jnp.int32, (ROWS, 2 * LANES), 1), ROWS
    )

    def new_tokens(g):
        queries = jnp.concatenate(
            [q_all[:, cols(g * CHUNK_COLS + h * DH, DH)] for h in range(HQ // HK)], axis=0
        )
        new_keys = q_all[:, cols(HQ * DH + g * DH, DH)]
        new_values = q_all[:, cols((HQ + HK) * DH + g * DH, DH)]
        top, total, weights = weigh(new_keys, queries, causal)
        summed = lax.dot_general(
            new_values, weights, (((0,), (0,)), ((), ())), preferred_element_type=jnp.float32
        )
        top = jnp.where(is_host, top, ABSENT)
        for half in range(2):
            lanes = slice(half * LANES, (half + 1) * LANES)
            new_sum[g, half] = summed[:, lanes]
            new_stats[g, half, 0:1] = top[:, lanes]
            new_stats[g, half, 1:2] = total[:, lanes]
        v_turned[g] = jnp.transpose(v_all[:, cols(g * DH, DH)])

    @pl.when(zhi == 0)
    def _():
        pl.semaphore_wait(barrier, 1)

    @pl.loop(0, CHUNKS)
    def _(s):
        for k in (1, 3, 2):
            send_y_q(s, k).wait_recv()
        z_q[s, zhi] = pick(host_y, [y_q[s, at] for at in range(NY)])
        send_z_q(s).start()
        new_tokens(s)

    valid = ctx_ref[0] - seq * context

    def attend(s, half):
        queries = jnp.concatenate([q_full[s, half, h] for h in range(NY)], axis=0)
        keep = lax.broadcasted_iota(jnp.int32, (context, LANES), 0) < valid
        top, total, weights = weigh(k_all[:, cols(s * DH, DH)], queries, keep)
        summed = jnp.dot(v_turned[s], weights, preferred_element_type=jnp.float32)
        new = (new_stats[s, half, 0:1], new_stats[s, half, 1:2], new_sum[s, half])
        return merge([(top, total, summed), new])

    def gather_q(s):
        send_z_q(s).wait_recv()
        q_full[s, core, y] = pick(host_z, [z_q[s, at] for at in range(2)])
        for k in (2, 1, 3):
            send_y_qall(s, k).start()

    def compute_near(s):
        for k in (1, 3, 2):
            send_y_qall(s, k).wait_recv()
        send_core_qall(s).start()
        top, total, summed = attend(s, core)
        o_src[s, 0:DH] = summed
        o_src[s, DH : DH + 1] = top
        o_src[s, DH + 1 : DH + 2] = total
        send_core_o(s).start()

    def compute_far(s):
        send_core_qall(s).wait_recv()
        part = attend(s, other)
        send_core_o(s).wait_recv()
        beside_it = (o_core[s, DH : DH + 1], o_core[s, DH + 1 : DH + 2], o_core[s, 0:DH])
        top, total, summed = merge([part, beside_it])
        packed = pack_stats(top, total)
        for piece in range(NY):
            block = piece // 2
            lanes = slice(block * BLOCK, (block + 1) * BLOCK)
            deep = summed[piece % 2 * DEPTH : (piece % 2 + 1) * DEPTH, lanes]
            y_osrc[s, piece, 0:DEPTH] = deep.astype(jnp.bfloat16)
            y_osrc[s, piece, DEPTH : DEPTH + 16] = packed[:, lanes]
            kept[s, piece, 0:DEPTH] = deep
            kept[s, piece, DEPTH : DEPTH + 1] = top[:, lanes]
            kept[s, piece, DEPTH + 1 : DEPTH + 2] = total[:, lanes]
        for k in (2, 1, 3):
            send_y_o(s, k).start()

    def arrived(ref, *at):
        top, total = unpack_stats(ref[(*at, slice(DEPTH, DEPTH + 16))])
        return top, total, ref[(*at, slice(0, DEPTH))].astype(jnp.float32)

    def sum_y(s):
        for k in (1, 3, 2):
            send_y_o(s, k).wait_recv()
        own = (kept[s, y, DEPTH : DEPTH + 1], kept[s, y, DEPTH + 1 : DEPTH + 2], kept[s, y, 0:DEPTH])
        top, total, summed = merge([own] + [arrived(y_o, s, y_of(k)) for k in (1, 2, 3)])
        z_osrc[s, 0:DEPTH] = summed.astype(jnp.bfloat16)
        z_osrc[s, DEPTH : DEPTH + 16] = pack_stats(top, total)
        send_z_o(s).start()
        half_o[s, 0:DEPTH] = summed
        half_o[s, DEPTH : DEPTH + 1] = top
        half_o[s, DEPTH + 1 : DEPTH + 2] = total

    def sent(single, along_y, s):
        for copy in single:
            copy(s).wait_send()
        for copy in along_y:
            for k in (1, 2, 3):
                copy(s, k).wait_send()

    def finish(s):
        sent((send_core_q, send_z_q, send_core_qall, send_core_o), (send_y_q, send_y_qall, send_y_o), s)
        send_z_o(s).wait_recv()
        own = (half_o[s, DEPTH : DEPTH + 1], half_o[s, DEPTH + 1 : DEPTH + 2], half_o[s, 0:DEPTH])
        _, total, summed = merge([own, arrived(z_o, s)])
        o_pieces[s, other, y] = (summed / total).astype(jnp.bfloat16)
        for k in (2, 1, 3):
            send_y_oall(s, k).start()

    def lay_out(s, half):
        for block in range(2):
            turned = jnp.transpose(
                jnp.concatenate([o_pieces[s, half, 2 * block + e].astype(jnp.float32) for e in range(2)], axis=0)
            ).astype(jnp.bfloat16)
            for h in range(2):
                o_full[s, :, cols(half * HALF_COLS + (2 * block + h) * DH, DH)] = turned[h * ROWS : (h + 1) * ROWS]

    def gather_o(s):
        for k in (1, 3, 2):
            send_y_oall(s, k).wait_recv()
        send_core_oall(s).start()
        lay_out(s, other)

    def write_o(s):
        send_core_oall(s).wait_recv()
        lay_out(s, core)
        write_out(s).start()
        sent((send_z_o, send_core_oall), (send_y_oall,), s)

    @pl.loop(0, CHUNKS + AT_WRITE)
    def _(t):
        for at, stage in (
            (0, gather_q),
            (AT_NEAR, compute_near),
            (AT_FAR, compute_far),
            (AT_SUM, sum_y),
            (AT_FINISH, finish),
            (AT_GATHER, gather_o),
            (AT_WRITE, write_o),
        ):
            pl.when((t >= at) & (t < at + CHUNKS))(functools.partial(stage, t - at))

    @pl.loop(0, CHUNKS)
    def _(s):
        write_out(s).wait()


def attention(query_block, keys, values, ctx_len, host):
    context, width = keys.shape
    bf16, f32 = jnp.bfloat16, jnp.float32
    vmem = pltpu.VMEM
    return pl.pallas_call(
        kernel,
        out_shape=jax.ShapeDtypeStruct((ROWS, HQ * DH), bf16),
        in_specs=[pl.BlockSpec(memory_space=pltpu.SMEM)] * 2 + [pl.BlockSpec(memory_space=pl.ANY)] * 3,
        out_specs=pl.BlockSpec(memory_space=pl.ANY),
        scratch_shapes=[
            vmem(query_block.shape, bf16),
            vmem((context, width), bf16),
            vmem((context, width), bf16),
            vmem((HK, DH, context), bf16),
            vmem((CHUNKS, 2, ROWS, HALF_COLS), bf16),
            vmem((CHUNKS, NY, ROWS, DH), bf16),
            vmem((CHUNKS, NY, ROWS, DH), bf16),
            vmem((CHUNKS, 2, ROWS, DH), bf16),
            vmem((CHUNKS, 2, NY, ROWS, DH), bf16),
            vmem((HK, 2, DH, LANES), f32),
            vmem((HK, 2, 8, LANES), f32),
            vmem((CHUNKS, DH + 8, LANES), f32),
            vmem((CHUNKS, DH + 8, LANES), f32),
            vmem((CHUNKS, NY, DEPTH + 8, BLOCK), f32),
            vmem((CHUNKS, NY, DEPTH + 16, BLOCK), bf16),
            vmem((CHUNKS, NY, DEPTH + 16, BLOCK), bf16),
            vmem((CHUNKS, DEPTH + 8, BLOCK), f32),
            vmem((CHUNKS, DEPTH + 16, BLOCK), bf16),
            vmem((CHUNKS, DEPTH + 16, BLOCK), bf16),
            vmem((CHUNKS, 2, NY, DEPTH, BLOCK), bf16),
            vmem((CHUNKS, ROWS, CHUNK_COLS), bf16),
            pltpu.SemaphoreType.DMA((4 + CHUNKS,)),
            pltpu.SemaphoreType.DMA((STAGES, CHUNKS)),
            pltpu.SemaphoreType.DMA((STAGES, CHUNKS)),
        ],
        compiler_params=pltpu.CompilerParams(
            collective_id=0, has_side_effects=True, vmem_limit_bytes=52 * 1024 * 1024
        ),
        name="context_attention",
    )(ctx_len, host, query_block, keys, values)


def local(query_block, k_cache, v_cache, ctx_len, host):
    result = attention(query_block[0, 0], k_cache[0], v_cache[0], ctx_len, host)
    result = jnp.where(lax.axis_index("seq") == host[0], result, jnp.zeros((), jnp.bfloat16))
    return result[None, None]


def solution(mesh):
    return jax.shard_map(
        local,
        mesh=mesh,
        in_specs=(
            P("req", "seq", None, None),
            P("req", "seq", None),
            P("req", "seq", None),
            P("req"),
            P("req"),
        ),
        out_specs=P("req", "seq", None, None),
        check_vma=False,
    )
```

time: 73.8 us -> 66.6 us (0.902)
  the two profiles are of different devices: /device:TPU:37 before, /device:TPU:193 now
where the time goes in v2:
time: 66.6 us; the launch traced here: 66.4 us
  Pallas kernels  64.1 us (96%)
  between operations  1.31 us (2%)
  other arithmetic  1.04 us (2%)
    pallas_call x1, Pallas kernels, attention(): pl.pallas_call(kernel, out_shape=jax.ShapeDtypeStruct((ROWS, HQ * DH), bf...  64.1 us

profile of v2, /device:TPU:193, one launch (start us, length us, event | category | flops | bytes accessed | tf_op | source)
XLA Modules:
  0.0 66.4 jit_solution(12750577124682405595)
XLA Ops:
  1.3 64.1 %context_attention.1 = bf16[64,8192]{1,0:T(8,128)(2,1)S(1)} custom-call(s32[1]{0:T(128)S(6)} %copy.6.ctx_ref, s32[1]{0:T(128)} %copy.7.host_ref, bf16[64,10240]{1,0:T(8,128)(2,1)} %bitcast.9, bf16[672,1024]{1,0:T(8,128)(2,1)} %bitcast.7, bf16[672,1024]{1,0:T(8,128)(2,1)} %bitcast.8), custom_call_target="tpu_custom_call" | custom-call | tf_op jit(solution)/shard_map/context_attention/pallas_call | solution.py:355
  65.4 1.0 %select_bitcast_fusion = bf16[1,1,64,8192]{3,2,1,0:T(8,128)(2,1)} fusion(bf16[64,8192]{1,0:T(8,128)(2,1)S(1)} %context_attention.1, pred[]{:T(512)S(6)} %eq.3), kind=kLoop, calls=%fused_computation | loop fusion | flops 524288 | bytes 2097153 | tf_op jit(solution)/shard_map/broadcast_in_dim | solution.py:396

commit v3 on v2

--- a/solution.py
+++ b/solution.py
@@ -26,8 +26,9 @@
 
 CORE_Q, Y_Q, Z_Q, Y_QALL, CORE_QALL, CORE_O, Y_O, Z_O, Y_OALL, CORE_OALL = 0, 1, 4, 5, 8, 9, 10, 13, 14, 17
 STAGES = 18
-
-AT_NEAR, AT_FAR, AT_SUM, AT_FINISH, AT_GATHER, AT_WRITE = 4, 5, 8, 16, 20, 22
+AHEAD = 4
+
+AT_NEAR, AT_FAR, AT_SUM, AT_FINISH, AT_GATHER, AT_WRITE = 4, 5, 8, 18, 24, 26
 
 
 def three_parts(x):
@@ -69,9 +70,9 @@
 
 
 def kernel(
-    ctx_ref, host_ref, q_hbm, k_hbm, v_hbm, o_hbm,
+    ctx_ref, host_ref, q_hbm, k_hbm, v_hbm, o_ref,
     q_all, k_all, v_all, v_turned, core_q, y_src, y_q, z_q, q_full,
-    new_sum, new_stats, o_src, o_core, kept, y_osrc, y_o, half_o, z_osrc, z_o, o_pieces, o_full,
+    new_sum, new_stats, o_src, o_core, kept, y_osrc, y_o, half_o, z_osrc, z_o, o_pieces,
     local_sem, send_sem, recv_sem,
 ):
     context = k_hbm.shape[0]
@@ -147,9 +148,6 @@
     def send_core_oall(s):
         return remote(o_pieces.at[s, other], o_pieces.at[s, other], CORE_OALL, s, sibling)
 
-    def write_out(s):
-        return pltpu.make_async_copy(o_full.at[s], o_hbm.at[:, cols(s * CHUNK_COLS, CHUNK_COLS)], local_sem.at[4 + s])
-
     def own_q(s):
         return pltpu.make_async_copy(
             q_hbm.at[:, cols(s * CHUNK_COLS + core * HALF_COLS, HALF_COLS)], core_q.at[s, core], local_sem.at[4 + s]
@@ -185,8 +183,7 @@
     def _(s):
         send_core_q(s).start()
 
-    @pl.loop(0, CHUNKS)
-    def _(s):
+    def turn_q(s):
         own_q(s).wait()
         send_core_q(s).wait_recv()
         for at in range(NY):
@@ -195,6 +192,8 @@
         for k in (2, 1, 3):
             send_y_q(s, k).start()
         y_q[s, y] = y_src[s, y]
+
+    pl.loop(0, AHEAD)(turn_q)
 
     for copy in loads:
         copy.wait()
@@ -231,6 +230,7 @@
             send_y_q(s, k).wait_recv()
         z_q[s, zhi] = pick(host_y, [y_q[s, at] for at in range(NY)])
         send_z_q(s).start()
+        pl.when(s + AHEAD < CHUNKS)(lambda: turn_q(s + AHEAD))
         new_tokens(s)
 
     valid = ctx_ref[0] - seq * context
@@ -316,7 +316,8 @@
                 jnp.concatenate([o_pieces[s, half, 2 * block + e].astype(jnp.float32) for e in range(2)], axis=0)
             ).astype(jnp.bfloat16)
             for h in range(2):
-                o_full[s, :, cols(half * HALF_COLS + (2 * block + h) * DH, DH)] = turned[h * ROWS : (h + 1) * ROWS]
+                start = s * CHUNK_COLS + half * HALF_COLS + (2 * block + h) * DH
+                o_ref[:, cols(start, DH)] = turned[h * ROWS : (h + 1) * ROWS]
 
     def gather_o(s):
         for k in (1, 3, 2):
@@ -327,7 +328,6 @@
     def write_o(s):
         send_core_oall(s).wait_recv()
         lay_out(s, core)
-        write_out(s).start()
         sent((send_z_o, send_core_oall), (send_y_oall,), s)
 
     @pl.loop(0, CHUNKS + AT_WRITE)
@@ -343,10 +343,6 @@
         ):
             pl.when((t >= at) & (t < at + CHUNKS))(functools.partial(stage, t - at))
 
-    @pl.loop(0, CHUNKS)
-    def _(s):
-        write_out(s).wait()
-
 
 def attention(query_block, keys, values, ctx_len, host):
     context, width = keys.shape
@@ -356,7 +352,7 @@
         kernel,
         out_shape=jax.ShapeDtypeStruct((ROWS, HQ * DH), bf16),
         in_specs=[pl.BlockSpec(memory_space=pltpu.SMEM)] * 2 + [pl.BlockSpec(memory_space=pl.ANY)] * 3,
-        out_specs=pl.BlockSpec(memory_space=pl.ANY),
+        out_specs=pl.BlockSpec(memory_space=pltpu.VMEM),
         scratch_shapes=[
             vmem(query_block.shape, bf16),
             vmem((context, width), bf16),
@@ -378,7 +374,6 @@
             vmem((CHUNKS, DEPTH + 16, BLOCK), bf16),
             vmem((CHUNKS, DEPTH + 16, BLOCK), bf16),
             vmem((CHUNKS, 2, NY, DEPTH, BLOCK), bf16),
-            vmem((CHUNKS, ROWS, CHUNK_COLS), bf16),
             pltpu.SemaphoreType.DMA((4 + CHUNKS,)),
             pltpu.SemaphoreType.DMA((STAGES, CHUNKS)),
             pltpu.SemaphoreType.DMA((STAGES, CHUNKS)),

time: 66.6 us -> 64.9 us (0.974)
  the two profiles are of different devices: /device:TPU:193 before, /device:TPU:161 now
where the time goes in v3:
time: 64.9 us; the launch traced here: 64.8 us
  Pallas kernels  62.4 us (96%)
  between operations  1.31 us (2%)
  other arithmetic  1.04 us (2%)
    pallas_call x1, Pallas kernels, attention(): pl.pallas_call(kernel, out_shape=jax.ShapeDtypeStruct((ROWS, HQ * DH), bf...  62.4 us

profile of v3, /device:TPU:161, one launch (start us, length us, event | category | flops | bytes accessed | tf_op | source)
XLA Modules:
  0.0 64.8 jit_solution(10134599836634432513)
XLA Ops:
  1.3 62.4 %context_attention.1 = bf16[64,8192]{1,0:T(8,128)(2,1)S(1)} custom-call(s32[1]{0:T(128)S(6)} %copy.6.ctx_ref, s32[1]{0:T(128)} %copy.7.host_ref, bf16[64,10240]{1,0:T(8,128)(2,1)} %bitcast.9, bf16[672,1024]{1,0:T(8,128)(2,1)} %bitcast.7, bf16[672,1024]{1,0:T(8,128)(2,1)} %bitcast.8), custom_call_target="tpu_custom_call" | custom-call | tf_op jit(solution)/shard_map/context_attention/pallas_call | solution.py:351
  63.7 1.0 %select_bitcast_fusion = bf16[1,1,64,8192]{3,2,1,0:T(8,128)(2,1)} fusion(bf16[64,8192]{1,0:T(8,128)(2,1)S(1)} %context_attention.1, pred[]{:T(512)S(6)} %eq.3), kind=kLoop, calls=%fused_computation | loop fusion | flops 524288 | bytes 2097153 | tf_op jit(solution)/shard_map/broadcast_in_dim | solution.py:391

commit v4 on v3

--- a/solution.py
+++ b/solution.py
@@ -28,7 +28,7 @@
 STAGES = 18
 AHEAD = 4
 
-AT_NEAR, AT_FAR, AT_SUM, AT_FINISH, AT_GATHER, AT_WRITE = 4, 5, 8, 18, 24, 26
+AT_NEAR, AT_FAR, AT_SUM, AT_FINISH, AT_GATHER, AT_WRITE = 4, 5, 8, 19, 25, 27
 
 
 def three_parts(x):
@@ -116,7 +116,7 @@
 
     def send_core_q(s):
         return remote(
-            q_hbm.at[:, cols(s * CHUNK_COLS + other * HALF_COLS, HALF_COLS)], core_q.at[s, core], CORE_Q, s, sibling
+            q_all.at[:, cols(s * CHUNK_COLS + other * HALF_COLS, HALF_COLS)], core_q.at[s], CORE_Q, s, sibling
         )
 
     def send_y_q(s, k):
@@ -147,11 +147,6 @@
 
     def send_core_oall(s):
         return remote(o_pieces.at[s, other], o_pieces.at[s, other], CORE_OALL, s, sibling)
-
-    def own_q(s):
-        return pltpu.make_async_copy(
-            q_hbm.at[:, cols(s * CHUNK_COLS + core * HALF_COLS, HALF_COLS)], core_q.at[s, core], local_sem.at[4 + s]
-        )
 
     loads = [
         pltpu.make_async_copy(src, dst, local_sem.at[at])
@@ -164,8 +159,6 @@
 
     for to in (beside(2), beside(1), beside(3), sibling):
         greet(to)
-    for s in range(CHUNKS):
-        own_q(s).start()
     for copy in loads:
         copy.start()
 
@@ -179,23 +172,24 @@
         pl.semaphore_wait(barrier, 5)
         greet(across)
 
+    loads[0].wait()
+
     @pl.loop(0, CHUNKS)
     def _(s):
         send_core_q(s).start()
 
     def turn_q(s):
-        own_q(s).wait()
         send_core_q(s).wait_recv()
         for at in range(NY):
-            piece = slice(at * DH, (at + 1) * DH)
-            y_src[s, at] = pick(host_core, [core_q[s, c, :, piece] for c in range(2)])
+            own = q_all[:, cols(s * CHUNK_COLS + core * HALF_COLS + at * DH, DH)]
+            y_src[s, at] = lax.select(host_core == core, own, core_q[s, :, at * DH : (at + 1) * DH])
         for k in (2, 1, 3):
             send_y_q(s, k).start()
         y_q[s, y] = y_src[s, y]
 
     pl.loop(0, AHEAD)(turn_q)
 
-    for copy in loads:
+    for copy in loads[1:]:
         copy.wait()
     is_host = jnp.broadcast_to(host, (1, 2 * LANES)) == jnp.broadcast_to(seq, (1, 2 * LANES))
     causal = lax.broadcasted_iota(jnp.int32, (ROWS, 2 * LANES), 0) <= lax.rem(
@@ -231,7 +225,6 @@
         z_q[s, zhi] = pick(host_y, [y_q[s, at] for at in range(NY)])
         send_z_q(s).start()
         pl.when(s + AHEAD < CHUNKS)(lambda: turn_q(s + AHEAD))
-        new_tokens(s)
 
     valid = ctx_ref[0] - seq * context
 
@@ -248,6 +241,11 @@
         q_full[s, core, y] = pick(host_z, [z_q[s, at] for at in range(2)])
         for k in (2, 1, 3):
             send_y_qall(s, k).start()
+
+        @pl.when(s < HK // 2)
+        def _():
+            new_tokens(2 * s)
+            new_tokens(2 * s + 1)
 
     def compute_near(s):
         for k in (1, 3, 2):
@@ -358,7 +356,7 @@
             vmem((context, width), bf16),
             vmem((context, width), bf16),
             vmem((HK, DH, context), bf16),
-            vmem((CHUNKS, 2, ROWS, HALF_COLS), bf16),
+            vmem((CHUNKS, ROWS, HALF_COLS), bf16),
             vmem((CHUNKS, NY, ROWS, DH), bf16),
             vmem((CHUNKS, NY, ROWS, DH), bf16),
             vmem((CHUNKS, 2, ROWS, DH), bf16),
@@ -374,7 +372,7 @@
             vmem((CHUNKS, DEPTH + 16, BLOCK), bf16),
             vmem((CHUNKS, DEPTH + 16, BLOCK), bf16),
             vmem((CHUNKS, 2, NY, DEPTH, BLOCK), bf16),
-            pltpu.SemaphoreType.DMA((4 + CHUNKS,)),
+            pltpu.SemaphoreType.DMA((3,)),
             pltpu.SemaphoreType.DMA((STAGES, CHUNKS)),
             pltpu.SemaphoreType.DMA((STAGES, CHUNKS)),
         ],

time: 64.9 us -> 64.8 us (level)
  the two profiles are of different devices: /device:TPU:161 before, /device:TPU:165 now
where the time goes in v4:
time: 64.8 us; the launch traced here: 64.6 us
  Pallas kernels  62.3 us (96%)
  between operations  1.31 us (2%)
  other arithmetic  1.04 us (2%)
    pallas_call x1, Pallas kernels, attention(): pl.pallas_call(kernel, out_shape=jax.ShapeDtypeStruct((ROWS, HQ * DH), bf...  62.3 us

profile of v4, /device:TPU:165, one launch (start us, length us, event | category | flops | bytes accessed | tf_op | source)
XLA Modules:
  0.0 64.6 jit_solution(6390738373217394920)
XLA Ops:
  1.3 62.3 %context_attention.1 = bf16[64,8192]{1,0:T(8,128)(2,1)S(1)} custom-call(s32[1]{0:T(128)S(6)} %copy.6.ctx_ref, s32[1]{0:T(128)} %copy.7.host_ref, bf16[64,10240]{1,0:T(8,128)(2,1)} %bitcast.9, bf16[672,1024]{1,0:T(8,128)(2,1)} %bitcast.7, bf16[672,1024]{1,0:T(8,128)(2,1)} %bitcast.8), custom_call_target="tpu_custom_call" | custom-call | tf_op jit(solution)/shard_map/context_attention/pallas_call | solution.py:349
  63.6 1.0 %select_bitcast_fusion = bf16[1,1,64,8192]{3,2,1,0:T(8,128)(2,1)} fusion(bf16[64,8192]{1,0:T(8,128)(2,1)S(1)} %context_attention.1, pred[]{:T(512)S(6)} %eq.3), kind=kLoop, calls=%fused_computation | loop fusion | flops 524288 | bytes 2097153 | tf_op jit(solution)/shard_map/broadcast_in_dim | solution.py:389

commit v5 on v3

--- a/solution.py
+++ b/solution.py
@@ -26,7 +26,7 @@
 
 CORE_Q, Y_Q, Z_Q, Y_QALL, CORE_QALL, CORE_O, Y_O, Z_O, Y_OALL, CORE_OALL = 0, 1, 4, 5, 8, 9, 10, 13, 14, 17
 STAGES = 18
-AHEAD = 4
+AHEAD = 5
 
 AT_NEAR, AT_FAR, AT_SUM, AT_FINISH, AT_GATHER, AT_WRITE = 4, 5, 8, 18, 24, 26
 
@@ -272,11 +272,14 @@
             deep = summed[piece % 2 * DEPTH : (piece % 2 + 1) * DEPTH, lanes]
             y_osrc[s, piece, 0:DEPTH] = deep.astype(jnp.bfloat16)
             y_osrc[s, piece, DEPTH : DEPTH + 16] = packed[:, lanes]
-            kept[s, piece, 0:DEPTH] = deep
+        for k in (2, 1, 3):
+            send_y_o(s, k).start()
+        for piece in range(NY):
+            block = piece // 2
+            lanes = slice(block * BLOCK, (block + 1) * BLOCK)
+            kept[s, piece, 0:DEPTH] = summed[piece % 2 * DEPTH : (piece % 2 + 1) * DEPTH, lanes]
             kept[s, piece, DEPTH : DEPTH + 1] = top[:, lanes]
             kept[s, piece, DEPTH + 1 : DEPTH + 2] = total[:, lanes]
-        for k in (2, 1, 3):
-            send_y_o(s, k).start()
 
     def arrived(ref, *at):
         top, total = unpack_stats(ref[(*at, slice(DEPTH, DEPTH + 16))])

time: 64.9 us -> 65.1 us (level)
  the two profiles are of different devices: /device:TPU:161 before, /device:TPU:193 now
where the time goes in v5:
time: 65.1 us; the launch traced here: 64.9 us
  Pallas kernels  62.6 us (96%)
  between operations  1.31 us (2%)
  other arithmetic  1.04 us (2%)
    pallas_call x1, Pallas kernels, attention(): pl.pallas_call(kernel, out_shape=jax.ShapeDtypeStruct((ROWS, HQ * DH), bf...  62.6 us

profile of v5, /device:TPU:193, one launch (start us, length us, event | category | flops | bytes accessed | tf_op | source)
XLA Modules:
  0.0 64.9 jit_solution(14831263295654209378)
XLA Ops:
  1.3 62.6 %context_attention.1 = bf16[64,8192]{1,0:T(8,128)(2,1)S(1)} custom-call(s32[1]{0:T(128)S(6)} %copy.6.ctx_ref, s32[1]{0:T(128)} %copy.7.host_ref, bf16[64,10240]{1,0:T(8,128)(2,1)} %bitcast.9, bf16[672,1024]{1,0:T(8,128)(2,1)} %bitcast.7, bf16[672,1024]{1,0:T(8,128)(2,1)} %bitcast.8), custom_call_target="tpu_custom_call" | custom-call | tf_op jit(solution)/shard_map/context_attention/pallas_call | solution.py:354
  63.9 1.0 %select_bitcast_fusion = bf16[1,1,64,8192]{3,2,1,0:T(8,128)(2,1)} fusion(bf16[64,8192]{1,0:T(8,128)(2,1)S(1)} %context_attention.1, pred[]{:T(512)S(6)} %eq.3), kind=kLoop, calls=%fused_computation | loop fusion | flops 524288 | bytes 2097153 | tf_op jit(solution)/shard_map/broadcast_in_dim | solution.py:394
